TPU v7x, 128 devices: a whole 4x4x4 slice. The times are simulated.
128 devices in a mesh: seq: 8 (over z, core), enc: 4 (over x), dp: 4 (over y).
Axes of the slice: x: 4, y: 4, z: 4, core: 2. Of those that a mesh axis runs over, the one named last changes fastest.
Arguments:
- tokens: bfloat16 [2048, 4096], P(('seq', 'enc', 'dp')), may hold values from -6 to 6
- cotangent: bfloat16 [2048, 4096], P(('seq', 'enc', 'dp')), may hold values from -6 to 6
- encoded: bfloat16 [128, 128, 4096], P('seq'), may hold values from -6 to 6
- w_query: bfloat16 [4096, 2048], P(None, ('enc', 'dp')), may hold values from -0.09375 to 0.09375
- w_key: bfloat16 [4096, 2048], P(None, ('enc', 'dp')), may hold values from -0.09375 to 0.09375
- w_value: bfloat16 [4096, 2048], P(None, ('enc', 'dp')), may hold values from -0.09375 to 0.09375
- w_out: bfloat16 [2048, 4096], P(('enc', 'dp')), may hold values from -0.5 to 0.5
- neigh_owner: int32 [32, 2], replicated, may hold values from 0 to 7, all different within a row; in each aligned block of 4 rows (0 to 3, 4 to 7, ...) at most 2 rows name the same one
- neigh_row: int32 [32, 2], replicated, may hold values from 0 to 15
Outputs:
- block_out: bfloat16 [2048, 4096], P(('seq', 'enc', 'dp'))
- grad_tokens: bfloat16 [2048, 4096], P(('seq', 'enc', 'dp'))
- grad_query: bfloat16 [4096, 2048], P('seq', ('enc', 'dp'))
- grad_key: bfloat16 [4096, 2048], P('seq', ('enc', 'dp'))
- grad_value: bfloat16 [4096, 2048], P('seq', ('enc', 'dp'))
- grad_out: bfloat16 [2048, 4096], P(('enc', 'dp'), 'seq')
Inputs may be any that keep to these rules, and one draw needn't show every extreme that they name: `neigh_owner`: the 2 owners of a group differ. Among the groups of one index of seq (aligned blocks of 4 rows) no owner is named more than 2 times, a bound that some block reaches.
All inputs are finite; a program needn't handle non-finite values.
Results may differ from a plain program's by a relative error of at most 0.02.
Values may be sent and summed in bfloat16 or wider, within the bound.
A program may use at most 128 MiB of HBM per device.

v0:
```python
import math

import jax
import jax.numpy as jnp
from jax import lax
from jax.sharding import PartitionSpec as P

GROUP = 64
SEQ_LEN = 2048


def request_plan(neigh_owner, neigh_row, seq_count, per_device):
    group_total = per_device + 1
    group_ids = (
        jnp.arange(seq_count, dtype=jnp.int32)[:, None] * per_device
        - 1
        + jnp.arange(group_total, dtype=jnp.int32)[None, :]
    )
    opening = jnp.arange(seq_count, dtype=jnp.int32) * per_device * GROUP % SEQ_LEN != 0
    needed = jnp.concatenate(
        [opening[:, None], jnp.ones((seq_count, per_device), dtype=bool)], axis=1
    )
    clipped = jnp.maximum(group_ids, 0)
    owners = jnp.where(needed[:, :, None], neigh_owner[clipped], -1).reshape(seq_count, -1)
    row_ids = neigh_row[clipped].reshape(seq_count, -1)
    onehot = (owners[:, :, None] == jnp.arange(seq_count, dtype=jnp.int32)[None, None, :]).astype(
        jnp.int32
    )
    before = jnp.cumsum(onehot, axis=1) - onehot
    slot_rank = jnp.sum(before * onehot, axis=2)
    return (owners, row_ids, slot_rank)


def attend(queries, kv_prev, kv_cur, last_row, live_mask):
    head_dim = queries.shape[-1]
    score_scale = 1.0 / math.sqrt(head_dim)
    pick = last_row[None, :, None]
    scores = (
        jnp.where(
            pick,
            jnp.einsum(
                "cqd,ckd->cqk", queries, kv_cur[..., :head_dim], preferred_element_type=jnp.float32
            ),
            jnp.einsum(
                "cqd,ckd->cqk", queries, kv_prev[..., :head_dim], preferred_element_type=jnp.float32
            ),
        )
        * score_scale
    )
    row_peak = jnp.max(scores, axis=-1, keepdims=True)
    expos = jnp.exp(scores - row_peak)
    attn_probs = expos / jnp.sum(expos, axis=-1, keepdims=True)
    probs_half = attn_probs.astype(jnp.bfloat16)
    mixed_vals = jnp.where(
        pick,
        jnp.einsum(
            "cqk,ckd->cqd", probs_half, kv_cur[..., head_dim:], preferred_element_type=jnp.float32
        ),
        jnp.einsum(
            "cqk,ckd->cqd", probs_half, kv_prev[..., head_dim:], preferred_element_type=jnp.float32
        ),
    )
    attn = (mixed_vals * live_mask[..., None]).astype(jnp.bfloat16)
    return (attn, attn_probs, probs_half)


def attend_back(queries, kv_prev, kv_cur, last_row, attn_probs, probs_half, d_attn):
    head_dim = queries.shape[-1]
    score_scale = 1.0 / math.sqrt(head_dim)
    pick = last_row[None, :, None]
    grad_probs = jnp.where(
        pick,
        jnp.einsum(
            "cqd,ckd->cqk", d_attn, kv_cur[..., head_dim:], preferred_element_type=jnp.float32
        ),
        jnp.einsum(
            "cqd,ckd->cqk", d_attn, kv_prev[..., head_dim:], preferred_element_type=jnp.float32
        ),
    )
    row_delta = jnp.sum(attn_probs * grad_probs, axis=-1, keepdims=True)
    d_scores = (attn_probs * (grad_probs - row_delta) * score_scale).astype(jnp.bfloat16)
    d_queries = jnp.where(
        pick,
        jnp.einsum(
            "cqk,ckd->cqd", d_scores, kv_cur[..., :head_dim], preferred_element_type=jnp.float32
        ),
        jnp.einsum(
            "cqk,ckd->cqd", d_scores, kv_prev[..., :head_dim], preferred_element_type=jnp.float32
        ),
    ).astype(jnp.bfloat16)
    last_half = last_row.astype(jnp.bfloat16)[None, :, None]
    other_half = (1 - last_row.astype(jnp.int32)).astype(jnp.bfloat16)[None, :, None]
    grad_prev = jnp.concatenate(
        [
            jnp.einsum(
                "cqk,cqd->ckd", d_scores * other_half, queries, preferred_element_type=jnp.float32
            ),
            jnp.einsum(
                "cqk,cqd->ckd", probs_half * other_half, d_attn, preferred_element_type=jnp.float32
            ),
        ],
        axis=-1,
    )
    grad_cur = jnp.concatenate(
        [
            jnp.einsum(
                "cqk,cqd->ckd", d_scores * last_half, queries, preferred_element_type=jnp.float32
            ),
            jnp.einsum(
                "cqk,cqd->ckd", probs_half * last_half, d_attn, preferred_element_type=jnp.float32
            ),
        ],
        axis=-1,
    )
    return (d_queries, grad_prev, grad_cur)


def split_pair(values):
    high_part = values.astype(jnp.bfloat16)
    low_part = (values - high_part.astype(jnp.float32)).astype(jnp.bfloat16)
    return jnp.concatenate([high_part, low_part], axis=-1)


def shards(tokens, cotangent, encoded, w_query, w_key, w_value, w_out, neigh_owner, neigh_row):
    seq_count = lax.axis_size("seq")
    per_device = neigh_owner.shape[0] // seq_count
    slot_count = min(per_device, max(2, 4 * per_device // seq_count)) + 1
    head_dim = w_query.shape[1]
    model_width = w_query.shape[0]
    blocks_own = encoded.shape[0]
    block_len = encoded.shape[1]
    seq_index = lax.axis_index("seq")
    whole_tokens, whole_grads = (
        lax.all_gather(tokens, ("enc", "dp"), axis=0, tiled=True),
        lax.all_gather(cotangent, ("enc", "dp"), axis=0, tiled=True),
    )
    owners, row_ids, slot_rank = request_plan(neigh_owner, neigh_row, seq_count, per_device)
    chosen = (owners[:, :, None] == seq_index) & (
        slot_rank[:, :, None] == jnp.arange(slot_count, dtype=jnp.int32)[None, None, :]
    )
    slot_rows = jnp.sum(jnp.where(chosen, row_ids[:, :, None], 0), axis=1)
    flat_rows = slot_rows.reshape(-1)
    w_pair = jnp.concatenate([w_key, w_value], axis=1)
    own_kv = jnp.dot(
        encoded.reshape(-1, model_width), w_pair, preferred_element_type=jnp.float32
    ).astype(jnp.bfloat16)
    slot_kv = own_kv.reshape(blocks_own, block_len * 2 * head_dim)[flat_rows]
    slot_kv = slot_kv.reshape(seq_count, slot_count, block_len, 2 * head_dim)
    fetched = lax.all_to_all(slot_kv, "seq", split_axis=0, concat_axis=0, tiled=True).reshape(
        seq_count * slot_count, block_len, 2 * head_dim
    )
    my_owner = owners[seq_index]
    my_slot = jnp.where(
        my_owner >= 0, my_owner * slot_count + slot_rank[seq_index], seq_count * slot_count
    )
    nearby = fetched[jnp.minimum(my_slot, seq_count * slot_count - 1)].reshape(
        per_device + 1, -1, 2 * head_dim
    )
    kv_prev = nearby[:-1]
    kv_cur = nearby[1:]
    group_ids = seq_index * per_device + jnp.arange(per_device, dtype=jnp.int32)
    positions = (group_ids[:, None] * GROUP + jnp.arange(GROUP, dtype=jnp.int32)[None, :]) % SEQ_LEN
    last_row = jnp.arange(GROUP, dtype=jnp.int32) == GROUP - 1
    live_mask = (last_row[None, :] | (positions >= GROUP)).astype(jnp.float32)
    queries = jnp.dot(whole_tokens, w_query, preferred_element_type=jnp.float32).astype(
        jnp.bfloat16
    )
    queries = queries.reshape(per_device, GROUP, head_dim)
    attn, attn_probs, probs_half = attend(queries, kv_prev, kv_cur, last_row, live_mask)
    attn_flat = attn.reshape(-1, head_dim)
    d_attn = lax.dot_general(
        whole_grads, w_out, (((1,), (1,)), ((), ())), preferred_element_type=jnp.float32
    )
    d_attn = (d_attn.reshape(per_device, GROUP, head_dim) * live_mask[..., None]).astype(
        jnp.bfloat16
    )
    d_queries, grad_prev, grad_cur = attend_back(
        queries, kv_prev, kv_cur, last_row, attn_probs, probs_half, d_attn
    )
    dq_flat = d_queries.reshape(-1, head_dim)
    zero_group = jnp.zeros_like(grad_prev[:1])
    grad_requests = jnp.concatenate([grad_prev, zero_group], axis=0) + jnp.concatenate(
        [zero_group, grad_cur], axis=0
    )
    grad_requests = grad_requests.reshape(-1, block_len, 2 * head_dim)
    outbound = jnp.zeros((seq_count * slot_count, block_len, 2 * head_dim), jnp.float32)
    outbound = outbound.at[my_slot].set(grad_requests, mode="drop")
    inbound = lax.all_to_all(
        outbound.reshape(seq_count, slot_count, block_len, 2 * head_dim).astype(jnp.bfloat16),
        "seq",
        split_axis=0,
        concat_axis=0,
        tiled=True,
    ).astype(jnp.float32)
    inbound = inbound.reshape(seq_count * slot_count, block_len * 2 * head_dim)
    member = (flat_rows[None, :] == jnp.arange(blocks_own, dtype=jnp.int32)[:, None]).astype(
        jnp.float32
    )
    summed = jnp.dot(
        member, inbound, precision=lax.Precision.HIGHEST, preferred_element_type=jnp.float32
    )
    halves = split_pair(summed.reshape(-1, 2 * head_dim))
    products = lax.dot_general(
        encoded.reshape(-1, model_width),
        halves,
        (((0,), (0,)), ((), ())),
        preferred_element_type=jnp.float32,
    )
    grad_kv = products[:, : 2 * head_dim] + products[:, 2 * head_dim :]
    grad_q = lax.dot_general(
        whole_tokens, dq_flat, (((0,), (0,)), ((), ())), preferred_element_type=jnp.float32
    )
    grad_o = lax.dot_general(
        whole_grads, attn_flat, (((0,), (0,)), ((), ())), preferred_element_type=jnp.float32
    )
    grad_sums = (
        lax.psum_scatter(
            grad_q.astype(jnp.bfloat16), "seq", scatter_dimension=0, tiled=True
        ).astype(jnp.float32),
        lax.psum_scatter(
            grad_kv[:, :head_dim].astype(jnp.bfloat16), "seq", scatter_dimension=0, tiled=True
        ).astype(jnp.float32),
        lax.psum_scatter(
            grad_kv[:, head_dim:].astype(jnp.bfloat16), "seq", scatter_dimension=0, tiled=True
        ).astype(jnp.float32),
        lax.psum_scatter(
            grad_o.astype(jnp.bfloat16), "seq", scatter_dimension=0, tiled=True
        ).astype(jnp.float32),
    )
    grad_query = grad_sums[0].astype(jnp.bfloat16)
    grad_key = grad_sums[1].astype(jnp.bfloat16)
    grad_value = grad_sums[2].astype(jnp.bfloat16)
    grad_out = grad_sums[3].T.astype(jnp.bfloat16)
    forward_part = jnp.dot(attn_flat, w_out, preferred_element_type=jnp.float32)
    backward_part = lax.dot_general(
        dq_flat, w_query, (((1,), (1,)), ((), ())), preferred_element_type=jnp.float32
    )
    head_total = lax.psum_scatter(
        jnp.concatenate([forward_part, backward_part], axis=1).astype(jnp.bfloat16),
        ("enc", "dp"),
        scatter_dimension=0,
        tiled=True,
    ).astype(jnp.float32)
    block_out = (tokens.astype(jnp.float32) + head_total[:, :model_width]).astype(jnp.bfloat16)
    grad_tokens = (cotangent.astype(jnp.float32) + head_total[:, model_width:]).astype(jnp.bfloat16)
    return (block_out, grad_tokens, grad_query, grad_key, grad_value, grad_out)


def solution(mesh):
    placed = (
        P(("seq", "enc", "dp"), None),
        P(("seq", "enc", "dp"), None),
        P("seq", None, None),
        P(None, ("enc", "dp")),
        P(None, ("enc", "dp")),
        P(None, ("enc", "dp")),
        P(("enc", "dp"), None),
        P(),
        P(),
    )
    return jax.shard_map(
        shards,
        mesh=mesh,
        in_specs=placed,
        out_specs=(
            P(("seq", "enc", "dp"), None),
            P(("seq", "enc", "dp"), None),
            P("seq", ("enc", "dp")),
            P("seq", ("enc", "dp")),
            P("seq", ("enc", "dp")),
            P(("enc", "dp"), "seq"),
        ),
        check_vma=False,
    )
```

profile of v0, /device:TPU:1, one launch (start us, length us, event | category | flops | bytes accessed | tf_op | source)
XLA Modules:
  0.0 356.1 jit_solution(7927181729179577897)
XLA Ops:
  13.7 11.0 %fusion.5 = bf16[2048,256]{0,1:T(8,128)(2,1)S(1)} fusion(bf16[2048,4096]{1,0:T(8,128)(2,1)} %bitcast.86, bf16[4096,128]{1,0:T(8,128)(2,1)} %param.14, bf16[4096,128]{1,0:T(8,128)(2,1)} %param.13), kind=kOutput, calls=%fused_computation.18 | convolution fusion | flops 4299685888 | bytes 19922944 | tf_op jit(solution)/shard_map/dot_general | solution.py:144
  25.8 2.7 gather_fusion.2
  28.6 2.9 copy.51
  31.5 6.8 %all-to-all-start = ((bf16[8,3,128,256]{3,2,1,0:T(8,128)(2,1)}), bf16[8,3,128,256]{3,2,1,0:T(8,128)(2,1)}, u32[]{:S(2)}, u32[]{:S(2)}) async-start(bf16[8,3,128,256]{3,2,1,0:T(8,128)(2,1)} %bitcast.24), calls=%async_computation | async-start | bytes 3145728 | tf_op jit(solution)/shard_map/all_to_all | solution.py:149
  40.0 19.2 %all-to-all-done = bf16[8,3,128,256]{3,2,1,0:T(8,128)(2,1)} async-done(((bf16[8,3,128,256]{3,2,1,0:T(8,128)(2,1)}), bf16[8,3,128,256]{3,2,1,0:T(8,128)(2,1)}, u32[]{:S(2)}, u32[]{:S(2)}) %all-to-all-start) | async-done | bytes 1572896 | tf_op jit(solution)/shard_map/all_to_all | solution.py:149
  59.1 2.0 gather_fusion.3
  62.0 2.5 fusion.99
  64.9 38.9 %all-gather.3.cloned.1.call-done = bf16[256,4096]{1,0:T(8,128)(2,1)} async-done(((bf16[16,4096]{1,0:T(8,128)(2,1)}), bf16[256,4096]{1,0:T(8,128)(2,1)}) %all-gather.3.cloned.1.call-update) | async-done | bytes 2097168 | tf_op jit(solution)/shard_map/all_gather | solution.py:134
  103.7 2.3 convolution_convert_fusion.5
  108.3 2.2 fusion.44
  110.5 3.0 fusion.40
  113.6 2.3 fusion.12
  115.8 1.7 copy.47
  117.5 2.0 broadcast_in_dim.97
  119.5 3.3 scatter_fusion
  122.9 3.3 convert_element_type.139
  126.2 6.0 %all-to-all-start.1 = ((bf16[8,3,128,256]{3,2,1,0:T(8,128)(2,1)}), bf16[8,3,128,256]{3,2,1,0:T(8,128)(2,1)}, u32[]{:S(2)}, u32[]{:S(2)}) async-start(bf16[8,3,128,256]{3,2,1,0:T(8,128)(2,1)} %bitcast.15), calls=%async_computation.3 | async-start | bytes 3145728 | tf_op jit(solution)/shard_map/all_to_all | solution.py:188
  132.8 2.8 fusion.34
  135.7 2.9 fusion.22
  138.5 2.3 fusion.2
  140.9 12.3 %all-to-all-done.1 = bf16[8,3,128,256]{3,2,1,0:T(8,128)(2,1)} async-done(((bf16[8,3,128,256]{3,2,1,0:T(8,128)(2,1)}), bf16[8,3,128,256]{3,2,1,0:T(8,128)(2,1)}, u32[]{:S(2)}, u32[]{:S(2)}) %all-to-all-start.1) | async-done | bytes 1572896 | tf_op jit(solution)/shard_map/all_to_all | solution.py:188
  153.2 2.3 copy.52
  155.5 1.8 fusion.68
  157.3 1.7 reshape.349
  159.3 11.7 %convolution_bitcast_fusion = f32[4096,512]{0,1:T(8,128)S(1)} fusion(bf16[2048,4096]{1,0:T(8,128)(2,1)} %bitcast.87, bf16[2048,256]{1,0:T(8,128)(2,1)S(1)} %get-tuple-element.24, bf16[2048,256]{1,0:T(8,128)(2,1)S(1)} %get-tuple-element.25), kind=kOutput, calls=%fused_computation.7 | convolution fusion | flops 8594128896 | bytes 27262976 | tf_op jit(solution)/shard_map/dot_general | solution.py:203
  175.9 2.4 pad_maximum_fusion
  181.4 1.8 copy.48
  183.2 19.1 %reduce-scatter.12.cloned.1.call-done = bf16[512,128]{0,1:T(8,128)(2,1)} async-done(((bf16[4096,128]{0,1:T(8,128)(2,1)}), bf16[512,128]{0,1:T(8,128)(2,1)}) %reduce-scatter.12.cloned.1.call-update) | async-done | bytes 131088 | tf_op jit(solution)/shard_map/reduce_scatter | solution.py:223
  202.3 1.7 copy.50
  203.9 31.4 %reduce-scatter.10.cloned.1.call-done = bf16[512,128]{0,1:T(8,128)(2,1)} async-done(((bf16[4096,128]{0,1:T(8,128)(2,1)}), bf16[512,128]{0,1:T(8,128)(2,1)}) %reduce-scatter.10.cloned.1.call-update) | async-done | bytes 131088 | tf_op jit(solution)/shard_map/reduce_scatter | solution.py:220
  237.0 79.0 %reduce-scatter.6.cloned.1.call-done = bf16[16,8192]{1,0:T(8,128)(2,1)} async-done(((bf16[256,8192]{1,0:T(8,128)(2,1)}), bf16[16,8192]{1,0:T(8,128)(2,1)}) %reduce-scatter.6.cloned.1.call-update) | async-done | bytes 262160 | tf_op jit(solution)/shard_map/reduce_scatter | solution.py:238
  317.8 31.5 %reduce-scatter.14.cloned.1.call-done = bf16[512,128]{0,1:T(8,128)(2,1)} async-done(((bf16[4096,128]{0,1:T(8,128)(2,1)}), bf16[512,128]{0,1:T(8,128)(2,1)}) %reduce-scatter.14.cloned.1.call-update) | async-done | bytes 131088 | tf_op jit(solution)/shard_map/reduce_scatter | solution.py:226
  (108 shorter events, 24.7 us)
Async XLA Ops:
  7.2 96.6 %copy-start = (bf16[4096,128]{1,0:T(8,128)(2,1)S(1)}, bf16[4096,128]{1,0:T(8,128)(2,1)}, u32[]{:S(2)}) copy-start(bf16[4096,128]{1,0:T(8,128)(2,1)} %param.12) | copy-start | bytes 3145732
  7.2 54.8 %all-gather.5.cloned.1.call-start = ((), (), s32[]{:S(2)}) async-start(), calls=%async_computation.8 | async-start | bytes 2228224 | tf_op jit(solution)/shard_map/all_gather | solution.py:135
  7.9 95.8 %all-gather.3.cloned.1.call-start = ((), (), s32[]{:S(2)}) async-start(), calls=%async_computation.7 | async-start | bytes 2228224 | tf_op jit(solution)/shard_map/all_gather | solution.py:134
  31.5 27.6 %all-to-all-start = ((bf16[8,3,128,256]{3,2,1,0:T(8,128)(2,1)}), bf16[8,3,128,256]{3,2,1,0:T(8,128)(2,1)}, u32[]{:S(2)}, u32[]{:S(2)}) async-start(bf16[8,3,128,256]{3,2,1,0:T(8,128)(2,1)} %bitcast.24), calls=%async_computation | async-start | bytes 3145728 | tf_op jit(solution)/shard_map/all_to_all | solution.py:149
  38.3 23.7 %copy-start.3 = (bf16[128,4096]{1,0:T(8,128)(2,1)S(1)}, bf16[128,4096]{1,0:T(8,128)(2,1)}, u32[]{:S(2)}) copy-start(bf16[128,4096]{1,0:T(8,128)(2,1)} %param.15) | copy-start | bytes 3145732
  62.0 45.1 %copy-start.5 = (bf16[8,128,256]{2,1,0:T(8,128)(2,1)}, bf16[8,128,256]{2,1,0:T(8,128)(2,1)S(1)}, u32[]{:S(2)}) copy-start(bf16[8,128,256]{2,1,0:T(8,128)(2,1)S(1)} %get-tuple-element.30) | copy-start | bytes 1572868
  62.0 2.6 copy-start.7
  106.0 1.7 copy-start.14
  106.0 2.0 copy-start.16
  107.5 3.0 copy-start.15
  117.5 2.0 copy-start.12
  126.2 27.0 %all-to-all-start.1 = ((bf16[8,3,128,256]{3,2,1,0:T(8,128)(2,1)}), bf16[8,3,128,256]{3,2,1,0:T(8,128)(2,1)}, u32[]{:S(2)}, u32[]{:S(2)}) async-start(bf16[8,3,128,256]{3,2,1,0:T(8,128)(2,1)} %bitcast.15), calls=%async_computation.3 | async-start | bytes 3145728 | tf_op jit(solution)/shard_map/all_to_all | solution.py:188
  132.2 6.3 %copy-start.2 = (bf16[256,4096]{1,0:T(8,128)(2,1)S(1)}, bf16[256,4096]{1,0:T(8,128)(2,1)}, u32[]{:S(2)}) copy-start(bf16[256,4096]{1,0:T(8,128)(2,1)} %all-gather.3.cloned.1.call-done) | copy-start | bytes 6291460
  132.2 49.2 %reduce-scatter.8.cloned.1.call-start = ((), (), s32[]{:S(2)}) async-start(), calls=%async_computation.10 | async-start | bytes 1179648 | tf_op jit(solution)/shard_map/reduce_scatter | solution.py:217
  140.8 14.6 %copy-start.13 = (s32[24]{0:T(128)S(1)}, s32[24]{0:T(128)}, u32[]{:S(2)}) copy-start(s32[24]{0:T(128)} %eq.102) | copy-start | bytes 292
  140.9 61.4 %reduce-scatter.12.cloned.1.call-start = ((), (), s32[]{:S(2)}) async-start(), calls=%async_computation.12 | async-start | bytes 1179648 | tf_op jit(solution)/shard_map/reduce_scatter | solution.py:223
  173.1 1.0 copy-start.8
  173.1 1.2 copy-start.6
  173.1 1.4 copy-start.11
  173.1 62.2 %reduce-scatter.10.cloned.1.call-start = ((), (), s32[]{:S(2)}) async-start(), calls=%async_computation.11 | async-start | bytes 1179648 | tf_op jit(solution)/shard_map/reduce_scatter | solution.py:220
  173.7 1.5 copy-start.4
  173.7 142.3 %reduce-scatter.6.cloned.1.call-start = ((), (), s32[]{:S(2)}) async-start(), calls=%async_computation.9 | async-start | bytes 4456448 | tf_op jit(solution)/shard_map/reduce_scatter | solution.py:238
  178.3 1.6 copy-start.1
  178.3 171.0 %reduce-scatter.14.cloned.1.call-start = ((), (), s32[]{:S(2)}) async-start(), calls=%async_computation.13 | async-start | bytes 1179648 | tf_op jit(solution)/shard_map/reduce_scatter | solution.py:226
  181.3 135.7 %copy-start.9 = (bf16[16,4096]{1,0:T(8,128)(2,1)S(1)}, bf16[16,4096]{1,0:T(8,128)(2,1)}, u32[]{:S(2)}) copy-start(bf16[16,4096]{1,0:T(8,128)(2,1)} %param.10) | copy-start | bytes 393220
  181.3 135.7 %copy-start.10 = (bf16[16,4096]{1,0:T(8,128)(2,1)S(1)}, bf16[16,4096]{1,0:T(8,128)(2,1)}, u32[]{:S(2)}) copy-start(bf16[16,4096]{1,0:T(8,128)(2,1)} %param.9) | copy-start | bytes 393220
Sparse Core Ops, SparseCore 0:
  10.2 47.1 all-gather.4
  59.5 44.1 all-gather.2
  141.0 30.0 reduce-scatter.7
  173.3 28.9 reduce-scatter.11
  204.5 30.7 reduce-scatter.9
  238.5 77.4 reduce-scatter.5
  319.1 30.1 reduce-scatter.13
where the time goes:
time: 359 us; the launch traced here: 356 us
  waiting for transfers between devices  233 us (65%)
  matrix products  48.1 us (13%)
  local copies, waits for them, and re-layouts  33.2 us (9%)
  between operations  14.5 us (4%)
  other arithmetic  13.9 us (4%)
  starting transfers between devices  13.1 us (4%)
    reduce_scatter x1, waiting for transfers between devices, shards(): lax.psum_scatter(jnp.concatenate([forward_part, backward_part], axis=1).a...  79 us
    all_gather x1, waiting for transfers between devices, shards(): lax.all_gather(tokens, ('enc', 'dp'), axis=0, tiled=True)  38.9 us
    reduce_scatter x1, waiting for transfers between devices, shards(): lax.psum_scatter(grad_o.astype(jnp.bfloat16), 'seq', scatter_dimension=0,...  31.5 us
    reduce_scatter x1, waiting for transfers between devices, shards(): lax.psum_scatter(grad_kv[:, :head_dim].astype(jnp.bfloat16), 'seq', scatt...  31.4 us
    all_to_all x1, waiting for transfers between devices, shards(): lax.all_to_all(slot_kv, 'seq', split_axis=0, concat_axis=0, tiled=True)  19.2 us
    reduce_scatter x1, waiting for transfers between devices, shards(): lax.psum_scatter(grad_kv[:, head_dim:].astype(jnp.bfloat16), 'seq', scatt...  19.1 us
    unnamed x41, local copies, waits for them, and re-layouts  13.8 us
    all_to_all x1, waiting for transfers between devices, shards(): lax.all_to_all(outbound.reshape(seq_count, slot_count, block_len, 2 * hea...  12.3 us
  transfers between devices with their start and end apart: 9, of which 7 were waited for; matrix products, arithmetic and copies ran while one was open for 20% of the time, Pallas kernels for 0%

commit v1 on v0

v1 whole, which is shorter than its diff:
```python
import math

import jax
import jax.numpy as jnp
from jax import lax
from jax.experimental import pallas as pl
from jax.experimental.pallas import tpu as pltpu
from jax.sharding import PartitionSpec as P

MESH = pl.DeviceIdType.MESH
BF = jnp.bfloat16
F32 = jnp.float32
D = 4096
HALF = D // 2
HEAD = 128
GROUP = 64
NSEQ = 8
RING = 4
TILE = D // NSEQ
MESSAGES = 188
SCALE = 1.0 / math.sqrt(HEAD)
NT = (((1,), (1,)), ((), ()))


def mm(a, b):
    return jnp.dot(a, b, preferred_element_type=F32)


def mm_t(a, b):
    return lax.dot_general(a, b, NT, preferred_element_type=F32)


class Link:
    def __init__(self, send, recv):
        self.send, self.recv, self.sent = send, recv, []

    def message(self, src, dst, peer, land):
        index = len(self.sent)
        out = pltpu.make_async_remote_copy(
            src_ref=src, dst_ref=dst, send_sem=self.send.at[index], recv_sem=self.recv.at[index],
            device_id=peer, device_id_type=MESH)
        back = pltpu.make_async_remote_copy(
            src_ref=land, dst_ref=land, send_sem=self.send.at[index], recv_sem=self.recv.at[index],
            device_id=peer, device_id_type=MESH)
        made = Message(out, back)
        self.sent.append(made)
        return made


class Message:
    def __init__(self, out, back):
        self.out, self.back = out, back

    def start(self):
        self.out.start()

    def wait(self):
        self.back.wait_recv()


class Gather:
    def __init__(self, link, axis, me, at, own=None):
        right, left, far = (me + 1) % RING, (me + 3) % RING, (me + 2) % RING
        own = own or (lambda h: at(me, h))
        to_r, to_l = {axis: right}, {axis: left}
        self.r = [link.message(own(h), at(me, h), to_r, at(left, h)) for h in (0, 1)]
        self.l = [link.message(own(h), at(me, h), to_l, at(right, h)) for h in (0, 1)]
        self.fr = link.message(at(left, 0), at(left, 0), to_r, at(far, 0))
        self.fl = link.message(at(right, 1), at(right, 1), to_l, at(far, 1))

    def start(self):
        self.r[0].start()
        self.l[1].start()
        self.r[1].start()
        self.l[0].start()

    def forward(self):
        self.r[0].wait()
        self.fr.start()
        self.l[1].wait()
        self.fl.start()

    def near(self):
        self.r[1].wait()
        self.l[0].wait()

    def far(self):
        self.fr.wait()
        self.fl.wait()


class Reduce:
    def __init__(self, link, axis, me, part, buf):
        right, left, far = (me + 1) % RING, (me + 3) % RING, (me + 2) % RING
        to_r, to_l = {axis: right}, {axis: left}
        self.me, self.right, self.left, self.part, self.buf = me, right, left, part, buf
        self.r2 = link.message(part(far, 0), buf(0), to_r, buf(0))
        self.r1b = link.message(part(right, 0), buf(1), to_r, buf(1))
        self.r1a = link.message(part(right, 1), buf(2), to_r, buf(2))
        self.l2 = link.message(part(far, 1), buf(3), to_l, buf(3))
        self.l1b = link.message(part(left, 1), buf(4), to_l, buf(4))
        self.l1a = link.message(part(left, 0), buf(5), to_l, buf(5))

    def start_far(self):
        self.r2.start()
        self.l2.start()

    def start_right(self):
        self.r1a.start()

    def start_left(self):
        self.l1a.start()

    def add(self, ref, *bufs):
        total = ref[...].astype(F32)
        for index in bufs:
            total = total + self.buf(index)[...].astype(F32)
        ref[...] = total.astype(BF)

    def middle(self):
        self.r2.wait()
        self.add(self.part(self.right, 0), 0)
        self.r1b.start()
        self.l2.wait()
        self.add(self.part(self.left, 1), 3)
        self.l1b.start()

    def arrive(self):
        self.r1a.wait()
        self.l1a.wait()
        self.r1b.wait()
        self.l1b.wait()

    def total(self, h):
        first, second = ((1, 5), (2, 4))[h]
        total = self.part(self.me, h)[...].astype(F32)
        return total + self.buf(first)[...].astype(F32) + self.buf(second)[...].astype(F32)

    def finish(self):
        self.arrive()
        for h in (0, 1):
            self.part(self.me, h)[...] = self.total(h).astype(BF)


def kernel(
    tok_h, cot_h, enc_h, wq_h, wk_h, wv_h, wo_h, owner, row_of,
    bo, gt, gq, gk, gv, go,
    enc, tok, cot, wq, wkv, wo, own_kv, kv_s, kv_r, qd, stats, ret_s, ret_r,
    fwd, bwd, rx, grad, core_in, rz, dkv_t, plan_row, plan_win, plan_use, slots,
    send, recv, local,
):
    S, X, Y = lax.axis_index("seq"), lax.axis_index("enc"), lax.axis_index("dp")
    Z, C = S // 2, S % 2
    other = Z * 2 + 1 - C
    link = Link(send, recv)

    copies = []

    def fetch(src, dst):
        copy = pltpu.make_async_copy(src, dst, local.at[len(copies)])
        copies.append(copy)
        copy.start()
        return copy

    barrier = pltpu.get_barrier_semaphore()
    peers = [{"enc": (X + 1) % RING}, {"enc": (X + 3) % RING}, {"dp": (Y + 1) % RING}, {"dp": (Y + 3) % RING}]
    peers += [{"seq": (S + d) % NSEQ} for d in range(1, NSEQ)]
    for peer in peers:
        pl.semaphore_signal(barrier, inc=1, device_id=peer, device_id_type=MESH)

    w_copies = [fetch(wk_h, wkv.at[:, pl.ds(0, HEAD)]), fetch(wv_h, wkv.at[:, pl.ds(HEAD, HEAD)])]
    e_copies = [fetch(enc_h.at[pl.ds(2 * c, 2)], enc.at[pl.ds(2 * c, 2)]) for c in range(8)]
    p_copies = [fetch(tok_h, tok.at[X, Y]), fetch(cot_h, cot.at[X, Y]), fetch(wq_h, wq), fetch(wo_h, wo)]

    pl.semaphore_wait(barrier, len(peers))

    def cols(h):
        return pl.ds(h * HALF, HALF)

    xr, xl, xo = (X + 1) % RING, (X + 3) % RING, (X + 2) % RING
    yr, yl, yo = (Y + 1) % RING, (Y + 3) % RING, (Y + 2) % RING
    t_own = lambda h: tok_h.at[:, cols(h)]
    c_own = lambda h: cot_h.at[:, cols(h)]
    tx = Gather(link, "enc", X, lambda p, h: tok.at[p, Y, :, cols(h)], t_own)
    cy = Gather(link, "dp", Y, lambda p, h: cot.at[X, p, :, cols(h)], c_own)
    ty = [
        Gather(link, "dp", Y, lambda p, h, b=b: tok.at[b, p, :, cols(h)], t_own if n == 0 else None)
        for n, b in enumerate((X, xl, xr, xo))
    ]
    cx = [
        Gather(link, "enc", X, lambda p, h, b=b: cot.at[p, b, :, cols(h)], c_own if n == 0 else None)
        for n, b in enumerate((Y, yl, yr, yo))
    ]
    tx.start()
    cy.start()
    ty[0].start()
    cx[0].start()

    def plan(d, carry):
        r = (S + d) % NSEQ
        count = jnp.int32(0)
        rows, wins, uses = [jnp.int32(0)] * 2, [jnp.int32(0)] * 2, [jnp.int32(0)] * 2
        for i in range(4):
            for j in range(2):
                hit = owner[4 * r + i, j] == S
                row = row_of[4 * r + i, j]
                for k in range(2):
                    here = jnp.logical_and(hit, count == k)
                    rows[k] = jnp.where(here, row, rows[k])
                    wins[k] = jnp.where(here, i, wins[k])
                    uses[k] = jnp.where(here, 1, uses[k])
                count = count + jnp.where(hit, 1, 0)
        for k in range(2):
            plan_row[2 * d + k] = rows[k]
            plan_win[2 * d + k] = wins[k]
            plan_use[2 * d + k] = uses[k]
        return carry

    lax.fori_loop(0, NSEQ, plan, 0)
    mine = []
    for i in range(4):
        for j in range(2):
            who = owner[4 * S + i, j]
            rank = jnp.int32(0)
            for before in mine:
                rank = rank + jnp.where(before == who, 1, 0)
            slots[2 * i + j] = who * 2 + rank
            mine.append(who)

    def project(c):
        e_copies[c].wait()
        total = None
        for k in range(4):
            part = mm(enc[2 * c:2 * c + 2, :, k * 1024:(k + 1) * 1024].reshape(256, 1024), wkv[k * 1024:(k + 1) * 1024, :])
            total = part if total is None else total + part
        own_kv[2 * c:2 * c + 2] = total.astype(BF).reshape(2, 128, 256)

    for copy in w_copies:
        copy.wait()
    project(0)
    tx.forward()
    cy.forward()
    project(1)
    tx.near()
    ty[1].start()
    ty[2].start()
    cy.near()
    cx[1].start()
    cx[2].start()
    project(2)
    ty[0].forward()
    cx[0].forward()
    project(3)
    tx.far()
    ty[3].start()
    cy.far()
    cx[3].start()
    project(4)
    project(5)
    ty[1].forward()
    cx[1].forward()
    project(6)
    project(7)
    kv_messages = []
    for d in range(1, NSEQ):
        for k in range(2):
            kv_s[2 * d + k] = own_kv[plan_row[2 * d + k]]
        message = link.message(
            kv_s.at[pl.ds(2 * d, 2)], kv_r.at[pl.ds(2 * S, 2)], {"seq": (S + d) % NSEQ},
            kv_r.at[pl.ds(2 * ((S + NSEQ - d) % NSEQ), 2)])
        message.start()
        kv_messages.append(message)
    for k in range(2):
        kv_r[2 * S + k] = own_kv[plan_row[k]]
    ty[2].forward()
    cx[2].forward()
    ty[3].forward()
    cx[3].forward()
    for copy in p_copies:
        copy.wait()
    for n in range(4):
        ty[n].near()
        cx[n].near()
        if n:
            ty[n - 1].far()
            cx[n - 1].far()
    ty[3].far()
    cx[3].far()

    q, da = None, None
    for k in range(4):
        ks = slice(k * 1024, (k + 1) * 1024)
        part = mm(tok[:, :, :, ks].reshape(256, 1024), wq[ks, :])
        q = part if q is None else q + part
        part = mm_t(cot[:, :, :, ks].reshape(256, 1024), wo[:, ks])
        da = part if da is None else da + part
    token = lax.broadcasted_iota(jnp.int32, (256, HEAD), 0)
    da = jnp.where(jnp.logical_or(token >= GROUP - 1, S > 0), da, 0.0)
    both = pltpu.roll(jnp.concatenate([q, da], axis=1), 1, 0).astype(BF)
    qd[pl.ds(4 * S, 4)] = both.reshape(4, GROUP, 256)

    def zb(p, h):
        return qd.at[pl.ds(4 * (2 * p + C) + 2 * h, 2)]

    def zo(p, h):
        return qd.at[pl.ds(4 * (2 * p + 1 - C) + 2 * h, 2)]

    zr, zl, zf = (Z + 1) % RING, (Z + 3) % RING, (Z + 2) % RING
    sibling = {"seq": other}

    class Column:
        pass

    def seq_peer(p):
        return {"seq": 2 * p + C}

    to_r, to_l = seq_peer(zr), seq_peer(zl)
    qg = Column()
    qg.r = [link.message(zb(Z, h), zb(Z, h), to_r, zb(zl, h)) for h in (0, 1)]
    qg.l = [link.message(zb(Z, h), zb(Z, h), to_l, zb(zr, h)) for h in (0, 1)]
    qg.fr = link.message(zb(zl, 0), zb(zl, 0), to_r, zb(zf, 0))
    qg.fl = link.message(zb(zr, 1), zb(zr, 1), to_l, zb(zf, 1))
    qs = {
        (p, h): link.message(zb(pos, h), zb(pos, h), sibling, zo(pos, h))
        for p, pos in (("me", Z), ("l", zl), ("r", zr), ("f", zf)) for h in (0, 1)
    }
    qg.l[0].start()
    qg.r[0].start()
    qg.l[1].start()
    qg.r[1].start()
    qs["me", 0].start()
    qs["me", 1].start()

    for message in kv_messages:
        message.wait()

    first_row = lax.broadcasted_iota(jnp.int32, (GROUP, 256), 0) == 0
    lane = lax.broadcasted_iota(jnp.int32, (GROUP, HEAD), 1)

    def window(i, pair):
        qw, dw = pair[:, :HEAD], pair[:, HEAD:]
        kv0, kv1 = kv_r[slots[2 * i]], kv_r[slots[2 * i + 1]]
        keys = jnp.concatenate([kv0[:, :HEAD], kv1[:, :HEAD]], axis=0)
        values = jnp.concatenate([kv0[:, HEAD:], kv1[:, HEAD:]], axis=0)
        scores = mm_t(qw, keys) * SCALE
        peak = jnp.max(scores, axis=-1, keepdims=True)
        expos = jnp.exp(scores - peak)
        norm = jnp.sum(expos, axis=-1, keepdims=True)
        probs = expos / norm
        out = mm(probs.astype(BF), values)
        d_probs = mm_t(dw, values)
        delta = jnp.sum(probs * d_probs, axis=-1, keepdims=True)
        d_scores = (probs * (d_probs - delta) * SCALE).astype(BF)
        dq = mm(d_scores, keys)
        column = jnp.where(lane == 0, peak + jnp.log(norm), delta)
        stats[4 * S + i] = jnp.concatenate([column, column], axis=0).T[:8, :]
        return jnp.concatenate([out, dq], axis=1)

    wins = [window(i, qd[4 * S + i + 1]) for i in range(3)]

    qg.l[0].wait()
    qg.r[0].wait()
    qg.fr.start()
    qs["r", 0].start()
    qg.l[1].wait()
    qg.fl.start()
    qg.r[1].wait()
    qs["r", 1].start()
    qs["l", 0].start()
    qs["l", 1].start()
    qs["me", 0].wait()
    qs["r", 0].wait()

    after = qd[(4 * S + 4) % 32].astype(F32)
    last = window(3, jnp.where(first_row, qd[4 * S].astype(F32), after).astype(BF))
    ret_s[...] = last.astype(BF)
    ret = link.message(ret_s, ret_r, {"seq": (S + 1) % NSEQ}, ret_r)
    ret.start()
    st_messages = []
    for d in range(1, NSEQ):
        message = link.message(
            stats.at[pl.ds(4 * S, 4)], stats.at[pl.ds(4 * S, 4)], {"seq": (S + d) % NSEQ},
            stats.at[pl.ds(4 * ((S + NSEQ - d) % NSEQ), 4)])
        message.start()
        st_messages.append(message)
    qg.fr.wait()
    qs["f", 0].start()
    qg.fl.wait()
    qs["f", 1].start()
    ret.wait()
    head = jnp.where(first_row, last, jnp.where(S > 0, ret_r[...].astype(F32), 0.0))
    done = pltpu.roll(jnp.concatenate([head] + wins, axis=0), 255, 0).astype(BF)
    attn, dq = done[:, :HEAD], done[:, HEAD:]

    for n in range(NSEQ):
        c = slice(n * TILE, (n + 1) * TILE)
        fwd[:, :, :, c] = mm(attn, wo[:, c]).astype(BF).reshape(4, 4, 16, TILE)
    ford = (xo, xr, xl, X)
    bord = (yo, yr, yl, Y)
    f1 = [
        Reduce(link, "dp", Y, lambda p, h, b=b: fwd.at[b, p, :, cols(h)], lambda k, n=n: rx.at[0, n, k])
        for n, b in enumerate(ford)
    ]
    b1 = [
        Reduce(link, "enc", X, lambda p, h, b=b: bwd.at[p, b, :, cols(h)], lambda k, n=n: rx.at[1, n, k])
        for n, b in enumerate(bord)
    ]
    f2 = Reduce(link, "enc", X, lambda p, h: fwd.at[p, Y, :, cols(h)], lambda k: rx.at[0, 4, k])
    b2 = Reduce(link, "dp", Y, lambda p, h: bwd.at[X, p, :, cols(h)], lambda k: rx.at[1, 4, k])

    def start(r):
        r.start_far()
        r.start_right()
        r.start_left()

    for r in f1:
        start(r)
    for n in range(NSEQ):
        c = slice(n * TILE, (n + 1) * TILE)
        bwd[:, :, :, c] = mm_t(dq, wq[c, :]).astype(BF).reshape(4, 4, 16, TILE)
    for r in b1:
        start(r)

    gc = [
        [
            link.message(grad.at[a, 2 * ((Z + w) % RING) + 1 - C], core_in.at[a, (Z + w) % RING], sibling, core_in.at[a, (Z + w) % RING])
            for w in (2, 1, 3, 0)
        ]
        for a in range(4)
    ]

    def zpart(a):
        return lambda p, h: grad.at[a, 2 * p + C, pl.ds(64 * h, 64), :]

    class ZReduce(Reduce):
        def __init__(self, a):
            part, buf = zpart(a), lambda k: rz.at[a, k]
            self.me, self.right, self.left, self.part, self.buf = Z, zr, zl, part, buf
            self.r2 = link.message(part(zf, 0), buf(0), to_r, buf(0))
            self.r1b = link.message(part(zr, 0), buf(1), to_r, buf(1))
            self.r1a = link.message(part(zr, 1), buf(2), to_r, buf(2))
            self.l2 = link.message(part(zf, 1), buf(3), to_l, buf(3))
            self.l1b = link.message(part(zl, 1), buf(4), to_l, buf(4))
            self.l1a = link.message(part(zl, 0), buf(5), to_l, buf(5))

    gz = [ZReduce(a) for a in range(4)]

    def core_sum(a, n):
        gc[a][n].wait()
        p = (Z + (2, 1, 3, 0)[n]) % RING
        total = grad[a, 2 * p + C].astype(F32) + core_in[a, p].astype(F32)
        grad[a, 2 * p + C] = total.astype(BF)
        if n == 0:
            gz[a].start_far()
        elif n == 1:
            gz[a].start_right()
        elif n == 2:
            gz[a].start_left()

    dq_t = dq.astype(F32).T.astype(BF)
    attn_t = attn.astype(F32).T.astype(BF)
    for n in range(NSEQ):
        c = slice(n * TILE, (n + 1) * TILE)
        grad[0, n] = mm(dq_t, tok[:, :, :, c].reshape(256, TILE)).astype(BF)
        grad[3, n] = mm(attn_t, cot[:, :, :, c].reshape(256, TILE)).astype(BF)
    for a in (0, 3):
        for n in range(4):
            gc[a][n].start()

    f1[0].middle()
    b1[0].middle()

    for p in "lf":
        for h in (0, 1):
            qs[p, h].wait()
    qs["me", 1].wait()
    qs["r", 1].wait()
    for message in st_messages:
        message.wait()

    def slot(d, k):
        index = 2 * d + k
        r = (S + d) % NSEQ
        b, i, use = plan_row[index], plan_win[index], plan_use[index]
        ahead = qd[(4 * r + i + 1) % 32].astype(F32)
        pair = jnp.where(jnp.logical_and(first_row, i == 3), qd[4 * r].astype(F32), ahead).astype(BF)
        qw, dw = pair[:, :HEAD], pair[:, HEAD:]
        kv = own_kv[b]
        stat = stats[4 * r + i]
        scores = mm_t(kv[:, :HEAD], qw) * SCALE
        probs = jnp.where(use > 0, jnp.exp(scores - stat[0:1, :GROUP]), 0.0)
        d_probs = mm_t(kv[:, HEAD:], dw)
        d_scores = probs * (d_probs - stat[1:2, :GROUP]) * SCALE
        d_keys = mm(d_scores.astype(BF), qw)
        d_values = mm(probs.astype(BF), dw)
        return jnp.concatenate([d_keys, d_values], axis=1).T.astype(BF)

    def slot_pair(d, carry):
        dkv_t[d] = jnp.concatenate([slot(d, 0), slot(d, 1)], axis=1)
        return carry

    lax.fori_loop(0, NSEQ, slot_pair, 0)
    f1[1].middle()
    b1[1].middle()

    def kv_tile(n):
        c = pl.ds(pl.multiple_of(n * TILE, TILE), TILE)
        total = None
        for d in range(NSEQ):
            rows = jnp.concatenate([enc[plan_row[2 * d], :, c], enc[plan_row[2 * d + 1], :, c]], axis=0)
            part = mm(dkv_t[d], rows)
            total = part if total is None else total + part
        total = total.astype(BF)
        grad[1, n] = total[:HEAD]
        grad[2, n] = total[HEAD:]

    for n, w in enumerate((2, 1, 3, 0)):
        kv_tile(2 * ((Z + w) % RING) + 1 - C)
        gc[1][n].start()
        gc[2][n].start()
        if n == 0:
            f1[2].middle()
            b1[2].middle()
        if n == 1:
            f1[3].middle()
            b1[3].middle()
        core_sum(0, n)
        core_sum(3, n)
    f1[0].finish()
    f2.start_far()
    b1[0].finish()
    b2.start_far()
    for n, w in enumerate((2, 1, 3, 0)):
        kv_tile(2 * ((Z + w) % RING) + C)
        core_sum(1, n)
        core_sum(2, n)
        if n == 0:
            gz[0].middle()
            gz[3].middle()
        if n == 1:
            f1[1].finish()
            f2.start_right()
            b1[1].finish()
            b2.start_right()
    f1[2].finish()
    f2.start_left()
    b1[2].finish()
    b2.start_left()
    f2.middle()
    b2.middle()
    gz[1].middle()
    gz[2].middle()
    f1[3].finish()
    b1[3].finish()

    gz[0].arrive()
    for h in (0, 1):
        gq[:, 64 * h:64 * h + 64] = gz[0].total(h).T.astype(BF)
    gz[3].arrive()
    for h in (0, 1):
        go[64 * h:64 * h + 64, :] = gz[3].total(h).astype(BF)
    f2.arrive()
    b2.arrive()
    for h in (0, 1):
        c = slice(h * HALF, (h + 1) * HALF)
        bo[:, c] = (tok[X, Y, :, c].astype(F32) + f2.total(h)).astype(BF)
        gt[:, c] = (cot[X, Y, :, c].astype(F32) + b2.total(h)).astype(BF)
    for a, ref in ((1, gk), (2, gv)):
        gz[a].arrive()
        for h in (0, 1):
            ref[:, 64 * h:64 * h + 64] = gz[a].total(h).T.astype(BF)
    for message in link.sent:
        message.out.wait_send()


def shards(tokens, cotangent, encoded, w_query, w_key, w_value, w_out, neigh_owner, neigh_row):
    any_ref = pl.BlockSpec(memory_space=pl.ANY)
    smem = pl.BlockSpec(memory_space=pltpu.SMEM)
    vmem = pl.BlockSpec(memory_space=pltpu.VMEM)
    shape = jax.ShapeDtypeStruct
    return pl.pallas_call(
        kernel,
        out_shape=(
            shape((16, D), BF), shape((16, D), BF), shape((TILE, HEAD), BF),
            shape((TILE, HEAD), BF), shape((TILE, HEAD), BF), shape((HEAD, TILE), BF),
        ),
        in_specs=[any_ref] * 7 + [smem] * 2,
        out_specs=(vmem,) * 6,
        scratch_shapes=[
            pltpu.VMEM((16, 128, D), BF),
            pltpu.VMEM((4, 4, 16, D), BF),
            pltpu.VMEM((4, 4, 16, D), BF),
            pltpu.VMEM((D, HEAD), BF),
            pltpu.VMEM((D, 2 * HEAD), BF),
            pltpu.VMEM((HEAD, D), BF),
            pltpu.VMEM((16, 128, 256), BF),
            pltpu.VMEM((16, 128, 256), BF),
            pltpu.VMEM((16, 128, 256), BF),
            pltpu.VMEM((32, GROUP, 256), BF),
            pltpu.VMEM((32, 8, 128), F32),
            pltpu.VMEM((GROUP, 256), BF),
            pltpu.VMEM((GROUP, 256), BF),
            pltpu.VMEM((4, 4, 16, D), BF),
            pltpu.VMEM((4, 4, 16, D), BF),
            pltpu.VMEM((2, 5, 6, 16, HALF), BF),
            pltpu.VMEM((4, NSEQ, HEAD, TILE), BF),
            pltpu.VMEM((4, 4, HEAD, TILE), BF),
            pltpu.VMEM((4, 6, 64, TILE), BF),
            pltpu.VMEM((NSEQ, 256, 256), BF),
            pltpu.SMEM((16,), jnp.int32),
            pltpu.SMEM((16,), jnp.int32),
            pltpu.SMEM((16,), jnp.int32),
            pltpu.SMEM((8,), jnp.int32),
            pltpu.SemaphoreType.DMA((MESSAGES + 8,)),
            pltpu.SemaphoreType.DMA((MESSAGES + 8,)),
            pltpu.SemaphoreType.DMA((16,)),
        ],
        compiler_params=pltpu.CompilerParams(
            collective_id=0, has_side_effects=True, vmem_limit_bytes=60 * 1024 * 1024
        ),
        cost_estimate=pl.CostEstimate(flops=10_500_000_000, bytes_accessed=22_000_000, transcendentals=400_000),
    )(tokens, cotangent, encoded, w_query, w_key, w_value, w_out, neigh_owner, neigh_row)


def solution(mesh):
    placed = (
        P(("seq", "enc", "dp"), None),
        P(("seq", "enc", "dp"), None),
        P("seq", None, None),
        P(None, ("enc", "dp")),
        P(None, ("enc", "dp")),
        P(None, ("enc", "dp")),
        P(("enc", "dp"), None),
        P(),
        P(),
    )
    return jax.shard_map(
        shards,
        mesh=mesh,
        in_specs=placed,
        out_specs=(
            P(("seq", "enc", "dp"), None),
            P(("seq", "enc", "dp"), None),
            P("seq", ("enc", "dp")),
            P("seq", ("enc", "dp")),
            P("seq", ("enc", "dp")),
            P(("enc", "dp"), "seq"),
        ),
        check_vma=False,
    )
```

time: 359 us -> 90.7 us (0.25)
  waiting for transfers between devices: 233 us -> 0 us
  Pallas kernels: 0 us -> 77.1 us
  matrix products: 48.1 us -> 0 us
  local copies, waits for them, and re-layouts: 33.2 us -> 12.1 us
  other arithmetic: 13.9 us -> 0 us
  between operations: 14.5 us -> 0.64 us
  starting transfers between devices: 13.1 us -> 0 us
    reduce_scatter x5 -> x0, waiting for transfers between devices: 161 us -> none  [the longest x1 79 us: shards(): lax.psum_scatter(jnp.concatenate([forward_part, backward_part], axis=1).a...]
    pallas_call x0 -> x1, Pallas kernels: none -> 77.1 us  [shards(): pl.pallas_call(kernel, out_shape=(shape((16, D), BF), shape((16, D), BF),...]
    dot_general x20 -> x0, matrix products: 47.7 us -> none  [the longest x1 11.7 us: shards(): lax.dot_general(encoded.reshape(-1, model_width), halves, (((0,), (0,)),...]
    all_gather x2 -> x0, waiting for transfers between devices: 38.9 us -> none  [the longest x1 38.9 us: shards(): lax.all_gather(tokens, ('enc', 'dp'), axis=0, tiled=True)]
    all_to_all x2 -> x0, waiting for transfers between devices: 31.4 us -> none  [the longest x1 19.2 us: shards(): lax.all_to_all(slot_kv, 'seq', split_axis=0, concat_axis=0, tiled=True)]
    all_to_all x2 -> x0, starting transfers between devices: 12.8 us -> none  [the longest x1 6.82 us: shards(): lax.all_to_all(slot_kv, 'seq', split_axis=0, concat_axis=0, tiled=True)]
    convert_element_type x10 -> x0, other arithmetic: 6.64 us -> none  [the longest x1 3.33 us: shards(): outbound.reshape(seq_count, slot_count, block_len, 2 * head_dim)]
    gather x6 -> x0, local copies, waits for them, and re-layouts: 6.04 us -> none  [the longest x1 2.73 us: shards(): slot_kv = own_kv.reshape(blocks_own, block_len * 2 * head_dim)[flat_rows]]
  transfers between devices with their start and end apart: 9 -> 0, of which waited for: 7 -> 0; matrix products, arithmetic and copies ran while one was open for 20% -> 0% of each run, Pallas kernels for 0% -> 0%
where the time goes in v1:
time: 90.7 us; the launch traced here: 89.9 us
  Pallas kernels  77.1 us (85%)
  local copies, waits for them, and re-layouts  12.1 us (13%)
    pallas_call x1, Pallas kernels, shards(): pl.pallas_call(kernel, out_shape=(shape((16, D), BF), shape((16, D), BF),...  77.1 us
    unnamed x8, local copies, waits for them, and re-layouts  12.1 us

profile of v1, /device:TPU:1, one launch (start us, length us, event | category | flops | bytes accessed | tf_op | source)
XLA Modules:
  0.0 89.9 jit_solution(10860293986231639182)
XLA Ops:
  0.6 1.4 %copy.15.owner = s32[32,2]{1,0:T(8,128)} copy(s32[32,2]{0,1:T(2,128)} %param.16) | data formatting | bytes 512 | tf_op args[7]
  2.0 1.4 %copy.16.row_of = s32[32,2]{1,0:T(8,128)} copy(s32[32,2]{0,1:T(2,128)} %param.17) | data formatting | bytes 512 | tf_op args[8]
  3.4 77.1 %shard_map.136 = (bf16[16,4096]{1,0:T(8,128)(2,1)}, bf16[16,4096]{1,0:T(8,128)(2,1)}, bf16[512,128]{1,0:T(8,128)(2,1)}, bf16[512,128]{1,0:T(8,128)(2,1)}, bf16[5...) custom-call(bf16[16,4096]{1,0:T(8,128)(2,1)} %tok_h.1, bf16[16,4096]{1,0:T(8,128)(2,1)} %cot_h.1, ...), custom_call_target="tpu_custom_call" | custom-call | flops 10499999744 | bytes 22000000 | tf_op jit(solution)/shard_map/pallas_call | solution.py:581
  80.4 1.6 %copy.23 = bf16[16,4096]{1,0:T(8,128)(2,1)} copy(bf16[16,4096]{1,0:T(8,128)(2,1)} %get-tuple-element.12) | data formatting | bytes 262144
  82.0 1.6 %copy.24 = bf16[16,4096]{1,0:T(8,128)(2,1)} copy(bf16[16,4096]{1,0:T(8,128)(2,1)} %get-tuple-element.13) | data formatting | bytes 262144
  83.6 1.6 %copy.25 = bf16[512,128]{1,0:T(8,128)(2,1)} copy(bf16[512,128]{1,0:T(8,128)(2,1)} %get-tuple-element.14) | data formatting | bytes 262144
  85.2 1.6 %copy.26 = bf16[512,128]{1,0:T(8,128)(2,1)} copy(bf16[512,128]{1,0:T(8,128)(2,1)} %get-tuple-element.15) | data formatting | bytes 262144
  86.7 1.6 %copy.27 = bf16[512,128]{1,0:T(8,128)(2,1)} copy(bf16[512,128]{1,0:T(8,128)(2,1)} %get-tuple-element.16) | data formatting | bytes 262144
  88.3 1.6 %copy.28 = bf16[128,512]{1,0:T(8,128)(2,1)} copy(bf16[128,512]{1,0:T(8,128)(2,1)} %get-tuple-element.17) | data formatting | bytes 262144

commit v2 on v1

--- a/solution.py
+++ b/solution.py
@@ -145,7 +145,7 @@
 def kernel(
     tok_h, cot_h, enc_h, wq_h, wk_h, wv_h, wo_h, owner, row_of,
     bo, gt, gq, gk, gv, go,
-    enc, tok, cot, wq, wkv, wo, own_kv, kv_s, kv_r, qd, stats, ret_s, ret_r,
+    enc, tok, cot, wq, wkv, wo, own_kv, kv_s, kv_r, qd, stats, prev_s, prev_r,
     fwd, bwd, rx, grad, core_in, rz, dkv_t, plan_row, plan_win, plan_use, slots,
     send, recv, local,
 ):
@@ -172,6 +172,47 @@
     e_copies = [fetch(enc_h.at[pl.ds(2 * c, 2)], enc.at[pl.ds(2 * c, 2)]) for c in range(8)]
     p_copies = [fetch(tok_h, tok.at[X, Y]), fetch(cot_h, cot.at[X, Y]), fetch(wq_h, wq), fetch(wo_h, wo)]
 
+    def plan(d, carry):
+        r = (S + d) % NSEQ
+        count = jnp.int32(0)
+        rows, wins, uses = [jnp.int32(0)] * 2, [jnp.int32(0)] * 2, [jnp.int32(0)] * 2
+        for i in range(4):
+            for j in range(2):
+                hit = owner[j, 4 * r + i] == S
+                row = row_of[j, 4 * r + i]
+                for k in range(2):
+                    here = jnp.logical_and(hit, count == k)
+                    rows[k] = jnp.where(here, row, rows[k])
+                    wins[k] = jnp.where(here, i, wins[k])
+                    uses[k] = jnp.where(here, 1, uses[k])
+                count = count + jnp.where(hit, 1, 0)
+        for k in range(2):
+            plan_row[2 * d + k] = rows[k]
+            plan_win[2 * d + k] = wins[k]
+            plan_use[2 * d + k] = uses[k]
+        return carry
+
+    lax.fori_loop(0, NSEQ, plan, 0)
+    mine = []
+    for i in range(4):
+        for j in range(2):
+            who = owner[j, 4 * S + i]
+            rank = jnp.int32(0)
+            for before in mine:
+                rank = rank + jnp.where(before == who, 1, 0)
+            slots[2 * i + j] = who * 2 + rank
+            mine.append(who)
+
+    def project(c):
+        e_copies[c].wait()
+        total = None
+        for k in range(4):
+            part = mm(enc[2 * c:2 * c + 2, :, k * 1024:(k + 1) * 1024].reshape(256, 1024), wkv[k * 1024:(k + 1) * 1024, :])
+            total = part if total is None else total + part
+        own_kv[2 * c:2 * c + 2] = total.astype(BF).reshape(2, 128, 256)
+
+    for copy in w_copies:
+        copy.wait()
     pl.semaphore_wait(barrier, len(peers))
 
     def cols(h):
@@ -196,70 +237,23 @@
     ty[0].start()
     cx[0].start()
 
-    def plan(d, carry):
-        r = (S + d) % NSEQ
-        count = jnp.int32(0)
-        rows, wins, uses = [jnp.int32(0)] * 2, [jnp.int32(0)] * 2, [jnp.int32(0)] * 2
-        for i in range(4):
-            for j in range(2):
-                hit = owner[4 * r + i, j] == S
-                row = row_of[4 * r + i, j]
-                for k in range(2):
-                    here = jnp.logical_and(hit, count == k)
-                    rows[k] = jnp.where(here, row, rows[k])
-                    wins[k] = jnp.where(here, i, wins[k])
-                    uses[k] = jnp.where(here, 1, uses[k])
-                count = count + jnp.where(hit, 1, 0)
-        for k in range(2):
-            plan_row[2 * d + k] = rows[k]
-            plan_win[2 * d + k] = wins[k]
-            plan_use[2 * d + k] = uses[k]
-        return carry
-
-    lax.fori_loop(0, NSEQ, plan, 0)
-    mine = []
-    for i in range(4):
-        for j in range(2):
-            who = owner[4 * S + i, j]
-            rank = jnp.int32(0)
-            for before in mine:
-                rank = rank + jnp.where(before == who, 1, 0)
-            slots[2 * i + j] = who * 2 + rank
-            mine.append(who)
-
-    def project(c):
-        e_copies[c].wait()
-        total = None
-        for k in range(4):
-            part = mm(enc[2 * c:2 * c + 2, :, k * 1024:(k + 1) * 1024].reshape(256, 1024), wkv[k * 1024:(k + 1) * 1024, :])
-            total = part if total is None else total + part
-        own_kv[2 * c:2 * c + 2] = total.astype(BF).reshape(2, 128, 256)
-
-    for copy in w_copies:
-        copy.wait()
     project(0)
+    project(1)
+    project(2)
+    project(3)
     tx.forward()
     cy.forward()
-    project(1)
+    project(4)
     tx.near()
     ty[1].start()
     ty[2].start()
     cy.near()
     cx[1].start()
     cx[2].start()
-    project(2)
+    project(5)
+    project(6)
     ty[0].forward()
     cx[0].forward()
-    project(3)
-    tx.far()
-    ty[3].start()
-    cy.far()
-    cx[3].start()
-    project(4)
-    project(5)
-    ty[1].forward()
-    cx[1].forward()
-    project(6)
     project(7)
     kv_messages = []
     for d in range(1, NSEQ):
@@ -272,12 +266,23 @@
         kv_messages.append(message)
     for k in range(2):
         kv_r[2 * S + k] = own_kv[plan_row[k]]
-    ty[2].forward()
-    cx[2].forward()
+    tx.far()
+    ty[3].start()
+    cy.far()
+    cx[3].start()
+    for n in (1, 2):
+        ty[n].forward()
+        cx[n].forward()
+    for copy in p_copies:
+        copy.wait()
     ty[3].forward()
     cx[3].forward()
-    for copy in p_copies:
-        copy.wait()
+    for message in kv_messages:
+        message.wait()
+    for j in range(2):
+        prev_s[j] = kv_r[slots[6 + j]]
+    before = link.message(prev_s, prev_r, {"seq": (S + 1) % NSEQ}, prev_r)
+    before.start()
     for n in range(4):
         ty[n].near()
         cx[n].near()
@@ -331,15 +336,12 @@
     qs["me", 0].start()
     qs["me", 1].start()
 
-    for message in kv_messages:
-        message.wait()
-
     first_row = lax.broadcasted_iota(jnp.int32, (GROUP, 256), 0) == 0
     lane = lax.broadcasted_iota(jnp.int32, (GROUP, HEAD), 1)
 
-    def window(i, pair):
+    def window(block, kv0, kv1):
+        pair = qd[4 * S + block]
         qw, dw = pair[:, :HEAD], pair[:, HEAD:]
-        kv0, kv1 = kv_r[slots[2 * i]], kv_r[slots[2 * i + 1]]
         keys = jnp.concatenate([kv0[:, :HEAD], kv1[:, :HEAD]], axis=0)
         values = jnp.concatenate([kv0[:, HEAD:], kv1[:, HEAD:]], axis=0)
         scores = mm_t(qw, keys) * SCALE
@@ -353,48 +355,22 @@
         d_scores = (probs * (d_probs - delta) * SCALE).astype(BF)
         dq = mm(d_scores, keys)
         column = jnp.where(lane == 0, peak + jnp.log(norm), delta)
-        stats[4 * S + i] = jnp.concatenate([column, column], axis=0).T[:8, :]
-        return jnp.concatenate([out, dq], axis=1)
-
-    wins = [window(i, qd[4 * S + i + 1]) for i in range(3)]
-
-    qg.l[0].wait()
-    qg.r[0].wait()
-    qg.fr.start()
-    qs["r", 0].start()
-    qg.l[1].wait()
-    qg.fl.start()
-    qg.r[1].wait()
-    qs["r", 1].start()
-    qs["l", 0].start()
-    qs["l", 1].start()
-    qs["me", 0].wait()
-    qs["r", 0].wait()
-
-    after = qd[(4 * S + 4) % 32].astype(F32)
-    last = window(3, jnp.where(first_row, qd[4 * S].astype(F32), after).astype(BF))
-    ret_s[...] = last.astype(BF)
-    ret = link.message(ret_s, ret_r, {"seq": (S + 1) % NSEQ}, ret_r)
-    ret.start()
-    st_messages = []
-    for d in range(1, NSEQ):
-        message = link.message(
-            stats.at[pl.ds(4 * S, 4)], stats.at[pl.ds(4 * S, 4)], {"seq": (S + d) % NSEQ},
-            stats.at[pl.ds(4 * ((S + NSEQ - d) % NSEQ), 4)])
-        message.start()
-        st_messages.append(message)
-    qg.fr.wait()
-    qs["f", 0].start()
-    qg.fl.wait()
-    qs["f", 1].start()
-    ret.wait()
-    head = jnp.where(first_row, last, jnp.where(S > 0, ret_r[...].astype(F32), 0.0))
-    done = pltpu.roll(jnp.concatenate([head] + wins, axis=0), 255, 0).astype(BF)
+        return jnp.concatenate([out, dq], axis=1), column
+
+    def publish(block, column):
+        stats[4 * S + block] = jnp.concatenate([column, column], axis=0).T[:8, :]
+
+    parts = [None] * 4
+    for i in range(3):
+        parts[i + 1], column = window(i + 1, kv_r[slots[2 * i]], kv_r[slots[2 * i + 1]])
+        publish(i + 1, column)
+    last, last_column = window(0, kv_r[slots[6]], kv_r[slots[7]])
+    before.wait()
+    early, early_column = window(0, prev_r[0], prev_r[1])
+    parts[0] = jnp.where(first_row, last, jnp.where(S > 0, early, 0.0))
+    publish(0, jnp.where(first_row[:, :HEAD], last_column, early_column))
+    done = pltpu.roll(jnp.concatenate(parts, axis=0), 255, 0).astype(BF)
     attn, dq = done[:, :HEAD], done[:, HEAD:]
-
-    for n in range(NSEQ):
-        c = slice(n * TILE, (n + 1) * TILE)
-        fwd[:, :, :, c] = mm(attn, wo[:, c]).astype(BF).reshape(4, 4, 16, TILE)
     ford = (xo, xr, xl, X)
     bord = (yo, yr, yl, Y)
     f1 = [
@@ -408,18 +384,39 @@
     f2 = Reduce(link, "enc", X, lambda p, h: fwd.at[p, Y, :, cols(h)], lambda k: rx.at[0, 4, k])
     b2 = Reduce(link, "dp", Y, lambda p, h: bwd.at[X, p, :, cols(h)], lambda k: rx.at[1, 4, k])
 
-    def start(r):
-        r.start_far()
-        r.start_right()
-        r.start_left()
-
-    for r in f1:
-        start(r)
-    for n in range(NSEQ):
-        c = slice(n * TILE, (n + 1) * TILE)
-        bwd[:, :, :, c] = mm_t(dq, wq[c, :]).astype(BF).reshape(4, 4, 16, TILE)
-    for r in b1:
-        start(r)
+    st_messages = []
+
+    def stats_and_queries():
+        for d in range(1, NSEQ):
+            message = link.message(
+                stats.at[pl.ds(4 * S, 4)], stats.at[pl.ds(4 * S, 4)], {"seq": (S + d) % NSEQ},
+                stats.at[pl.ds(4 * ((S + NSEQ - d) % NSEQ), 4)])
+            message.start()
+            st_messages.append(message)
+
+    def head_sum(ref, rings, h, tile):
+        for n in range(4 * h, 4 * h + 4):
+            c = slice(n * TILE, (n + 1) * TILE)
+            ref[:, :, :, c] = tile(c).astype(BF).reshape(4, 4, 16, TILE)
+        for r in rings:
+            (r.l2 if h else r.r2).start()
+            (r.r1a if h else r.l1a).start()
+
+    stats_and_queries()
+    for h in (0, 1):
+        head_sum(fwd, f1, h, lambda c: mm(attn, wo[:, c]))
+        head_sum(bwd, b1, h, lambda c: mm_t(dq, wq[c, :]))
+        if h == 0:
+            qg.l[0].wait()
+            qs["r", 0].start()
+            qg.r[0].wait()
+            qg.fr.start()
+            qg.l[1].wait()
+            qg.fl.start()
+            qg.r[1].wait()
+            qs["r", 1].start()
+            qs["l", 0].start()
+            qs["l", 1].start()
 
     gc = [
         [
@@ -457,26 +454,34 @@
         elif n == 2:
             gz[a].start_left()
 
-    dq_t = dq.astype(F32).T.astype(BF)
-    attn_t = attn.astype(F32).T.astype(BF)
-    for n in range(NSEQ):
-        c = slice(n * TILE, (n + 1) * TILE)
-        grad[0, n] = mm(dq_t, tok[:, :, :, c].reshape(256, TILE)).astype(BF)
-        grad[3, n] = mm(attn_t, cot[:, :, :, c].reshape(256, TILE)).astype(BF)
-    for a in (0, 3):
+    def token_gradient(a, left, right):
+        left_t = left.astype(F32).T.astype(BF)
+        for n in range(NSEQ):
+            c = slice(n * TILE, (n + 1) * TILE)
+            grad[a, n] = mm(left_t, right[:, :, :, c].reshape(256, TILE)).astype(BF)
         for n in range(4):
             gc[a][n].start()
 
+    token_gradient(3, attn, cot)
+    qg.fr.wait()
+    qs["f", 0].start()
+    qg.fl.wait()
+    qs["f", 1].start()
+    token_gradient(0, dq, tok)
     f1[0].middle()
     b1[0].middle()
-
-    for p in "lf":
-        for h in (0, 1):
-            qs[p, h].wait()
-    qs["me", 1].wait()
-    qs["r", 1].wait()
+    for n in range(4):
+        core_sum(3, n)
+    f1[1].middle()
+    b1[1].middle()
+    for n in range(4):
+        core_sum(0, n)
+    for message in qs.values():
+        message.wait()
     for message in st_messages:
         message.wait()
+
+    first_lane = lax.broadcasted_iota(jnp.int32, (8, HEAD), 1) == 0
 
     def slot(d, k):
         index = 2 * d + k
@@ -486,7 +491,7 @@
         pair = jnp.where(jnp.logical_and(first_row, i == 3), qd[4 * r].astype(F32), ahead).astype(BF)
         qw, dw = pair[:, :HEAD], pair[:, HEAD:]
         kv = own_kv[b]
-        stat = stats[4 * r + i]
+        stat = jnp.where(jnp.logical_and(first_lane, i == 3), stats[4 * r], stats[(4 * r + i + 1) % 32])
         scores = mm_t(kv[:, :HEAD], qw) * SCALE
         probs = jnp.where(use > 0, jnp.exp(scores - stat[0:1, :GROUP]), 0.0)
         d_probs = mm_t(kv[:, HEAD:], dw)
@@ -500,8 +505,11 @@
         return carry
 
     lax.fori_loop(0, NSEQ, slot_pair, 0)
-    f1[1].middle()
-    b1[1].middle()
+    gz[3].middle()
+    f1[2].middle()
+    b1[2].middle()
+    f1[3].middle()
+    b1[3].middle()
 
     def kv_tile(n):
         c = pl.ds(pl.multiple_of(n * TILE, TILE), TILE)
@@ -518,26 +526,17 @@
         kv_tile(2 * ((Z + w) % RING) + 1 - C)
         gc[1][n].start()
         gc[2][n].start()
-        if n == 0:
-            f1[2].middle()
-            b1[2].middle()
-        if n == 1:
-            f1[3].middle()
-            b1[3].middle()
-        core_sum(0, n)
-        core_sum(3, n)
-    f1[0].finish()
-    f2.start_far()
-    b1[0].finish()
-    b2.start_far()
-    for n, w in enumerate((2, 1, 3, 0)):
         kv_tile(2 * ((Z + w) % RING) + C)
         core_sum(1, n)
         core_sum(2, n)
         if n == 0:
             gz[0].middle()
-            gz[3].middle()
-        if n == 1:
+        if n == 2:
+            f1[0].finish()
+            f2.start_far()
+            b1[0].finish()
+            b2.start_far()
+        if n == 3:
             f1[1].finish()
             f2.start_right()
             b1[1].finish()
@@ -573,12 +572,25 @@
         message.out.wait_send()
 
 
+def deliver(*refs):
+    inputs, outputs, held, sems = refs[:6], refs[6:12], refs[12:18], refs[18]
+    into = [pltpu.make_async_copy(inputs[n], held[n], sems.at[n]) for n in range(6)]
+    out = [pltpu.make_async_copy(held[n], outputs[n], sems.at[6 + n]) for n in range(6)]
+    for copy in into:
+        copy.start()
+    for n in range(6):
+        into[n].wait()
+        out[n].start()
+    for copy in out:
+        copy.wait()
+
+
 def shards(tokens, cotangent, encoded, w_query, w_key, w_value, w_out, neigh_owner, neigh_row):
     any_ref = pl.BlockSpec(memory_space=pl.ANY)
     smem = pl.BlockSpec(memory_space=pltpu.SMEM)
     vmem = pl.BlockSpec(memory_space=pltpu.VMEM)
     shape = jax.ShapeDtypeStruct
-    return pl.pallas_call(
+    results = pl.pallas_call(
         kernel,
         out_shape=(
             shape((16, D), BF), shape((16, D), BF), shape((TILE, HEAD), BF),
@@ -598,8 +610,8 @@
             pltpu.VMEM((16, 128, 256), BF),
             pltpu.VMEM((32, GROUP, 256), BF),
             pltpu.VMEM((32, 8, 128), F32),
-            pltpu.VMEM((GROUP, 256), BF),
-            pltpu.VMEM((GROUP, 256), BF),
+            pltpu.VMEM((2, 128, 256), BF),
+            pltpu.VMEM((2, 128, 256), BF),
             pltpu.VMEM((4, 4, 16, D), BF),
             pltpu.VMEM((4, 4, 16, D), BF),
             pltpu.VMEM((2, 5, 6, 16, HALF), BF),
@@ -619,7 +631,15 @@
             collective_id=0, has_side_effects=True, vmem_limit_bytes=60 * 1024 * 1024
         ),
         cost_estimate=pl.CostEstimate(flops=10_500_000_000, bytes_accessed=22_000_000, transcendentals=400_000),
-    )(tokens, cotangent, encoded, w_query, w_key, w_value, w_out, neigh_owner, neigh_row)
+    )(tokens, cotangent, encoded, w_query, w_key, w_value, w_out, neigh_owner.T, neigh_row.T)
+    return pl.pallas_call(
+        deliver,
+        out_shape=tuple(shape(r.shape, r.dtype) for r in results),
+        in_specs=[any_ref] * 6,
+        out_specs=(any_ref,) * 6,
+        scratch_shapes=[pltpu.VMEM(r.shape, r.dtype) for r in results] + [pltpu.SemaphoreType.DMA((12,))],
+        compiler_params=pltpu.CompilerParams(vmem_limit_bytes=60 * 1024 * 1024),
+    )(*results)
 
 
 def solution(mesh):

time: 90.7 us -> 77.2 us (0.85)
  local copies, waits for them, and re-layouts: 12.1 us -> 0 us
    unnamed x8 -> x0, local copies, waits for them, and re-layouts: 12.1 us -> none
    pallas_call x1, Pallas kernels: 77.1 us -> 74.2 us  [shards(): pl.pallas_call(kernel, out_shape=(shape((16, D), BF), shape((16, D), BF),...]
    pallas_call x0 -> x1, Pallas kernels: none -> 1.97 us  [shards(): pl.pallas_call(deliver, out_shape=tuple((shape(r.shape, r.dtype) for r in...]
where the time goes in v2:
time: 77.2 us; the launch traced here: 77 us
  Pallas kernels  76.2 us (99%)
  between operations  0.8 us (1%)
    pallas_call x1, Pallas kernels, shards(): pl.pallas_call(kernel, out_shape=(shape((16, D), BF), shape((16, D), BF),...  74.2 us
    pallas_call x1, Pallas kernels, shards(): pl.pallas_call(deliver, out_shape=tuple((shape(r.shape, r.dtype) for r in...  1.97 us

profile of v2, /device:TPU:1, one launch (start us, length us, event | category | flops | bytes accessed | tf_op | source)
XLA Modules:
  0.0 77.0 jit_solution(12538013818410099207)
XLA Ops:
  0.6 74.2 %shard_map.136 = (bf16[16,4096]{1,0:T(8,128)(2,1)}, bf16[16,4096]{1,0:T(8,128)(2,1)}, bf16[512,128]{1,0:T(8,128)(2,1)}, bf16[512,128]{1,0:T(8,128)(2,1)}, bf16[5...) custom-call(bf16[16,4096]{1,0:T(8,128)(2,1)} %tok_h.1, bf16[16,4096]{1,0:T(8,128)(2,1)} %cot_h.1, ...), custom_call_target="tpu_custom_call" | custom-call | flops 10499999744 | bytes 22000000 | tf_op jit(solution)/shard_map/pallas_call | solution.py:593
  74.9 2.0 %shard_map.137 = (bf16[16,4096]{1,0:T(8,128)(2,1)}, bf16[16,4096]{1,0:T(8,128)(2,1)}, bf16[512,128]{1,0:T(8,128)(2,1)}, bf16[512,128]{1,0:T(8,128)(2,1)}, bf16[5...) custom-call(bf16[16,4096]{1,0:T(8,128)(2,1)} %get-tuple-element.12.refs_0_, bf16[16,4096]{1,0:T(8,128)(2,1)} %get-tuple-element.13.refs_1_, ...), custom_call_target="tpu_custom_call" | custom-call | tf_op jit(solution)/shard_map/pallas_call | solution.py:635

commit v3 on v2

--- a/solution.py
+++ b/solution.py
@@ -34,6 +34,12 @@
     def __init__(self, send, recv):
         self.send, self.recv, self.sent = send, recv, []
 
+    def drain(self):
+        for message in self.sent:
+            if message.pending:
+                message.pending = False
+                message.out.wait_send()
+
     def message(self, src, dst, peer, land):
         index = len(self.sent)
         out = pltpu.make_async_remote_copy(
@@ -50,8 +56,10 @@
 class Message:
     def __init__(self, out, back):
         self.out, self.back = out, back
+        self.pending = False
 
     def start(self):
+        self.pending = True
         self.out.start()
 
     def wait(self):
@@ -144,10 +152,10 @@
 
 def kernel(
     tok_h, cot_h, enc_h, wq_h, wk_h, wv_h, wo_h, owner, row_of,
-    bo, gt, gq, gk, gv, go,
-    enc, tok, cot, wq, wkv, wo, own_kv, kv_s, kv_r, qd, stats, prev_s, prev_r,
+    bo_h, gt_h, gq_h, gk_h, gv_h, go_h,
+    enc, tok, cot, wq, wkv, wo, own_kv, kv_s, kv_r, qd, stats, prev_s, prev_r, q_rows, d_rows,
     fwd, bwd, rx, grad, core_in, rz, dkv_t, plan_row, plan_win, plan_use, slots,
-    send, recv, local,
+    bo, gt, gq, gk, gv, go, send, recv, local,
 ):
     S, X, Y = lax.axis_index("seq"), lax.axis_index("enc"), lax.axis_index("dp")
     Z, C = S // 2, S % 2
@@ -289,16 +297,28 @@
         if n:
             ty[n - 1].far()
             cx[n - 1].far()
+
+    def project_rows(xs, ys):
+        q, da = None, None
+        for k in range(4):
+            ks = slice(k * 1024, (k + 1) * 1024)
+            rows = jnp.concatenate([tok[b, :, :, ks].reshape(GROUP, 1024) for b in xs], axis=0)
+            part = mm(rows, wq[ks, :])
+            q = part if q is None else q + part
+            rows = jnp.concatenate([cot[:, b, :, ks].reshape(GROUP, 1024) for b in ys], axis=0)
+            part = mm_t(rows, wo[:, ks])
+            da = part if da is None else da + part
+        for n, b in enumerate(xs):
+            q_rows[b] = q[GROUP * n:GROUP * (n + 1)].reshape(4, 16, HEAD)
+        for n, b in enumerate(ys):
+            d_rows[:, b] = da[GROUP * n:GROUP * (n + 1)].reshape(4, 16, HEAD)
+
+    project_rows((X, xl, xr), (Y, yl, yr))
     ty[3].far()
     cx[3].far()
 
-    q, da = None, None
-    for k in range(4):
-        ks = slice(k * 1024, (k + 1) * 1024)
-        part = mm(tok[:, :, :, ks].reshape(256, 1024), wq[ks, :])
-        q = part if q is None else q + part
-        part = mm_t(cot[:, :, :, ks].reshape(256, 1024), wo[:, ks])
-        da = part if da is None else da + part
+    project_rows((xo,), (yo,))
+    q, da = q_rows[...].reshape(256, HEAD), d_rows[...].reshape(256, HEAD)
     token = lax.broadcasted_iota(jnp.int32, (256, HEAD), 0)
     da = jnp.where(jnp.logical_or(token >= GROUP - 1, S > 0), da, 0.0)
     both = pltpu.roll(jnp.concatenate([q, da], axis=1), 1, 0).astype(BF)
@@ -400,6 +420,7 @@
             ref[:, :, :, c] = tile(c).astype(BF).reshape(4, 4, 16, TILE)
         for r in rings:
             (r.l2 if h else r.r2).start()
+        for r in rings[:1]:
             (r.r1a if h else r.l1a).start()
 
     stats_and_queries()
@@ -418,6 +439,8 @@
             qs["l", 0].start()
             qs["l", 1].start()
 
+    early = [m for m in link.sent if m.pending and m not in [r.r2 for r in f1 + b1] + [r.l2 for r in f1 + b1] + [r.r1a for r in f1 + b1] + [r.l1a for r in f1 + b1]]
+
     gc = [
         [
             link.message(grad.at[a, 2 * ((Z + w) % RING) + 1 - C], core_in.at[a, (Z + w) % RING], sibling, core_in.at[a, (Z + w) % RING])
@@ -470,6 +493,9 @@
     token_gradient(0, dq, tok)
     f1[0].middle()
     b1[0].middle()
+    for r in (f1[1], b1[1], f1[2], b1[2], f1[3], b1[3]):
+        r.start_right()
+        r.start_left()
     for n in range(4):
         core_sum(3, n)
     f1[1].middle()
@@ -508,8 +534,6 @@
     gz[3].middle()
     f1[2].middle()
     b1[2].middle()
-    f1[3].middle()
-    b1[3].middle()
 
     def kv_tile(n):
         c = pl.ds(pl.multiple_of(n * TILE, TILE), TILE)
@@ -536,6 +560,8 @@
             f2.start_far()
             b1[0].finish()
             b2.start_far()
+            f1[3].middle()
+            b1[3].middle()
         if n == 3:
             f1[1].finish()
             f2.start_right()
@@ -545,6 +571,9 @@
     f2.start_left()
     b1[2].finish()
     b2.start_left()
+    for message in early:
+        message.pending = False
+        message.out.wait_send()
     f2.middle()
     b2.middle()
     gz[1].middle()
@@ -555,21 +584,27 @@
     gz[0].arrive()
     for h in (0, 1):
         gq[:, 64 * h:64 * h + 64] = gz[0].total(h).T.astype(BF)
+    fetch(gq, gq_h)
     gz[3].arrive()
     for h in (0, 1):
         go[64 * h:64 * h + 64, :] = gz[3].total(h).astype(BF)
+    fetch(go, go_h)
     f2.arrive()
     b2.arrive()
     for h in (0, 1):
         c = slice(h * HALF, (h + 1) * HALF)
         bo[:, c] = (tok[X, Y, :, c].astype(F32) + f2.total(h)).astype(BF)
         gt[:, c] = (cot[X, Y, :, c].astype(F32) + b2.total(h)).astype(BF)
-    for a, ref in ((1, gk), (2, gv)):
+    fetch(bo, bo_h)
+    fetch(gt, gt_h)
+    for a, ref, whole in ((1, gk, gk_h), (2, gv, gv_h)):
         gz[a].arrive()
         for h in (0, 1):
             ref[:, 64 * h:64 * h + 64] = gz[a].total(h).T.astype(BF)
-    for message in link.sent:
-        message.out.wait_send()
+        fetch(ref, whole)
+    link.drain()
+    for copy in copies[14:]:
+        copy.wait()
 
 
 def deliver(*refs):
@@ -588,7 +623,6 @@
 def shards(tokens, cotangent, encoded, w_query, w_key, w_value, w_out, neigh_owner, neigh_row):
     any_ref = pl.BlockSpec(memory_space=pl.ANY)
     smem = pl.BlockSpec(memory_space=pltpu.SMEM)
-    vmem = pl.BlockSpec(memory_space=pltpu.VMEM)
     shape = jax.ShapeDtypeStruct
     results = pl.pallas_call(
         kernel,
@@ -597,7 +631,7 @@
             shape((TILE, HEAD), BF), shape((TILE, HEAD), BF), shape((HEAD, TILE), BF),
         ),
         in_specs=[any_ref] * 7 + [smem] * 2,
-        out_specs=(vmem,) * 6,
+        out_specs=(any_ref,) * 6,
         scratch_shapes=[
             pltpu.VMEM((16, 128, D), BF),
             pltpu.VMEM((4, 4, 16, D), BF),
@@ -612,6 +646,8 @@
             pltpu.VMEM((32, 8, 128), F32),
             pltpu.VMEM((2, 128, 256), BF),
             pltpu.VMEM((2, 128, 256), BF),
+            pltpu.VMEM((4, 4, 16, HEAD), F32),
+            pltpu.VMEM((4, 4, 16, HEAD), F32),
             pltpu.VMEM((4, 4, 16, D), BF),
             pltpu.VMEM((4, 4, 16, D), BF),
             pltpu.VMEM((2, 5, 6, 16, HALF), BF),
@@ -623,9 +659,15 @@
             pltpu.SMEM((16,), jnp.int32),
             pltpu.SMEM((16,), jnp.int32),
             pltpu.SMEM((8,), jnp.int32),
+            pltpu.VMEM((16, D), BF),
+            pltpu.VMEM((16, D), BF),
+            pltpu.VMEM((TILE, HEAD), BF),
+            pltpu.VMEM((TILE, HEAD), BF),
+            pltpu.VMEM((TILE, HEAD), BF),
+            pltpu.VMEM((HEAD, TILE), BF),
             pltpu.SemaphoreType.DMA((MESSAGES + 8,)),
             pltpu.SemaphoreType.DMA((MESSAGES + 8,)),
-            pltpu.SemaphoreType.DMA((16,)),
+            pltpu.SemaphoreType.DMA((24,)),
         ],
         compiler_params=pltpu.CompilerParams(
             collective_id=0, has_side_effects=True, vmem_limit_bytes=60 * 1024 * 1024

time: 77.2 us -> 73.4 us (0.951)
  Pallas kernels: 76.2 us -> 72.4 us
    pallas_call x1, Pallas kernels: 74.2 us -> 70.5 us  [shards(): pl.pallas_call(kernel, out_shape=(shape((16, D), BF), shape((16, D), BF),...]
where the time goes in v3:
time: 73.4 us; the launch traced here: 73.2 us
  Pallas kernels  72.4 us (99%)
  between operations  0.8 us (1%)
    pallas_call x1, Pallas kernels, shards(): pl.pallas_call(kernel, out_shape=(shape((16, D), BF), shape((16, D), BF),...  70.5 us
    pallas_call x1, Pallas kernels, shards(): pl.pallas_call(deliver, out_shape=tuple((shape(r.shape, r.dtype) for r in...  1.97 us

profile of v3, /device:TPU:1, one launch (start us, length us, event | category | flops | bytes accessed | tf_op | source)
XLA Modules:
  0.0 73.2 jit_solution(7565407917214070868)
XLA Ops:
  0.6 70.5 %shard_map.136 = (bf16[16,4096]{1,0:T(8,128)(2,1)}, bf16[16,4096]{1,0:T(8,128)(2,1)}, bf16[512,128]{1,0:T(8,128)(2,1)}, bf16[512,128]{1,0:T(8,128)(2,1)}, bf16[5...) custom-call(bf16[16,4096]{1,0:T(8,128)(2,1)} %tok_h.1, bf16[16,4096]{1,0:T(8,128)(2,1)} %cot_h.1, ...), custom_call_target="tpu_custom_call" | custom-call | flops 10499999744 | bytes 22000000 | tf_op jit(solution)/shard_map/pallas_call | solution.py:627
  71.1 2.0 %shard_map.137 = (bf16[16,4096]{1,0:T(8,128)(2,1)}, bf16[16,4096]{1,0:T(8,128)(2,1)}, bf16[512,128]{1,0:T(8,128)(2,1)}, bf16[512,128]{1,0:T(8,128)(2,1)}, bf16[5...) custom-call(bf16[16,4096]{1,0:T(8,128)(2,1)} %get-tuple-element.12.refs_0_, bf16[16,4096]{1,0:T(8,128)(2,1)} %get-tuple-element.13.refs_1_, ...), custom_call_target="tpu_custom_call" | custom-call | tf_op jit(solution)/shard_map/pallas_call | solution.py:677

commit v4 on v3

--- a/solution.py
+++ b/solution.py
@@ -555,22 +555,23 @@
         core_sum(2, n)
         if n == 0:
             gz[0].middle()
-        if n == 2:
+        if n == 1:
             f1[0].finish()
             f2.start_far()
             b1[0].finish()
             b2.start_far()
             f1[3].middle()
             b1[3].middle()
-        if n == 3:
+        if n == 2:
             f1[1].finish()
             f2.start_right()
             b1[1].finish()
             b2.start_right()
-    f1[2].finish()
-    f2.start_left()
-    b1[2].finish()
-    b2.start_left()
+        if n == 3:
+            f1[2].finish()
+            f2.start_left()
+            b1[2].finish()
+            b2.start_left()
     for message in early:
         message.pending = False
         message.out.wait_send()

time: 73.4 us -> 71.7 us (0.977)
  Pallas kernels: 72.4 us -> 70.7 us
    pallas_call x1, Pallas kernels: 70.5 us -> 68.8 us  [shards(): pl.pallas_call(kernel, out_shape=(shape((16, D), BF), shape((16, D), BF),...]
where the time goes in v4:
time: 71.7 us; the launch traced here: 71.6 us
  Pallas kernels  70.7 us (99%)
  between operations  0.8 us (1%)
    pallas_call x1, Pallas kernels, shards(): pl.pallas_call(kernel, out_shape=(shape((16, D), BF), shape((16, D), BF),...  68.8 us
    pallas_call x1, Pallas kernels, shards(): pl.pallas_call(deliver, out_shape=tuple((shape(r.shape, r.dtype) for r in...  1.97 us

profile of v4, /device:TPU:1, one launch (start us, length us, event | category | flops | bytes accessed | tf_op | source)
XLA Modules:
  0.0 71.6 jit_solution(11882516808001191644)
XLA Ops:
  0.6 68.8 %shard_map.136 = (bf16[16,4096]{1,0:T(8,128)(2,1)}, bf16[16,4096]{1,0:T(8,128)(2,1)}, bf16[512,128]{1,0:T(8,128)(2,1)}, bf16[512,128]{1,0:T(8,128)(2,1)}, bf16[5...) custom-call(bf16[16,4096]{1,0:T(8,128)(2,1)} %tok_h.1, bf16[16,4096]{1,0:T(8,128)(2,1)} %cot_h.1, ...), custom_call_target="tpu_custom_call" | custom-call | flops 10499999744 | bytes 22000000 | tf_op jit(solution)/shard_map/pallas_call | solution.py:628
  69.4 2.0 %shard_map.137 = (bf16[16,4096]{1,0:T(8,128)(2,1)}, bf16[16,4096]{1,0:T(8,128)(2,1)}, bf16[512,128]{1,0:T(8,128)(2,1)}, bf16[512,128]{1,0:T(8,128)(2,1)}, bf16[5...) custom-call(bf16[16,4096]{1,0:T(8,128)(2,1)} %get-tuple-element.12.refs_0_, bf16[16,4096]{1,0:T(8,128)(2,1)} %get-tuple-element.13.refs_1_, ...), custom_call_target="tpu_custom_call" | custom-call | tf_op jit(solution)/shard_map/pallas_call | solution.py:678

commit v5 on v4

--- a/solution.py
+++ b/solution.py
@@ -555,19 +555,19 @@
         core_sum(2, n)
         if n == 0:
             gz[0].middle()
-        if n == 1:
+        if n == 0:
             f1[0].finish()
             f2.start_far()
             b1[0].finish()
             b2.start_far()
             f1[3].middle()
             b1[3].middle()
-        if n == 2:
+        if n == 1:
             f1[1].finish()
             f2.start_right()
             b1[1].finish()
             b2.start_right()
-        if n == 3:
+        if n == 2:
             f1[2].finish()
             f2.start_left()
             b1[2].finish()

time: 71.7 us -> 71.4 us (level)
  no operation moved by 1% of the time
where the time goes in v5:
time: 71.4 us; the launch traced here: 71.3 us
  Pallas kernels  70.4 us (99%)
  between operations  0.8 us (1%)
    pallas_call x1, Pallas kernels, shards(): pl.pallas_call(kernel, out_shape=(shape((16, D), BF), shape((16, D), BF),...  68.5 us
    pallas_call x1, Pallas kernels, shards(): pl.pallas_call(deliver, out_shape=tuple((shape(r.shape, r.dtype) for r in...  1.97 us

profile of v5, /device:TPU:1, one launch (start us, length us, event | category | flops | bytes accessed | tf_op | source)
XLA Modules:
  0.0 71.3 jit_solution(7145063042334304791)
XLA Ops:
  0.6 68.5 %shard_map.136 = (bf16[16,4096]{1,0:T(8,128)(2,1)}, bf16[16,4096]{1,0:T(8,128)(2,1)}, bf16[512,128]{1,0:T(8,128)(2,1)}, bf16[512,128]{1,0:T(8,128)(2,1)}, bf16[5...) custom-call(bf16[16,4096]{1,0:T(8,128)(2,1)} %tok_h.1, bf16[16,4096]{1,0:T(8,128)(2,1)} %cot_h.1, ...), custom_call_target="tpu_custom_call" | custom-call | flops 10499999744 | bytes 22000000 | tf_op jit(solution)/shard_map/pallas_call | solution.py:628
  69.1 2.0 %shard_map.137 = (bf16[16,4096]{1,0:T(8,128)(2,1)}, bf16[16,4096]{1,0:T(8,128)(2,1)}, bf16[512,128]{1,0:T(8,128)(2,1)}, bf16[512,128]{1,0:T(8,128)(2,1)}, bf16[5...) custom-call(bf16[16,4096]{1,0:T(8,128)(2,1)} %get-tuple-element.12.refs_0_, bf16[16,4096]{1,0:T(8,128)(2,1)} %get-tuple-element.13.refs_1_, ...), custom_call_target="tpu_custom_call" | custom-call | tf_op jit(solution)/shard_map/pallas_call | solution.py:678
